TPU v7x, 256 devices: a whole 4x4x8 slice. The times are simulated.
256 devices in a mesh: shard: 64 (over z, x, core), grp: 4 (over y).
Axes of the slice: x: 4, y: 4, z: 8, core: 2. Of those that a mesh axis runs over, the one named last changes fastest.
Arguments:
- embed: bfloat16 [131072, 768], P(('shard', 'grp')), may hold values from -700 to 700
- cluster: int32 [131072, 1], P(('shard', 'grp')), may hold values from 0 to 63; in each aligned block of 512 rows (0 to 511, 512 to 1023, ...) at most 16 rows name the same one
Outputs:
- nearest_earlier: float32 [131072], P(('shard', 'grp'))
Inputs may be any that keep to these rules, and one draw needn't show every extreme that they name: Within the rows of one device, no cluster occurs more than 16 times.
All inputs are finite; a program needn't handle non-finite values.
Results may differ from a plain program's by a relative error of at most 0.0014.
Values may be sent and summed in bfloat16 or wider, within the bound.
A program may use at most 64 MiB of HBM per device.

v0:
```python
import math

import jax
import jax.numpy as jnp
from jax import lax
from jax.sharding import PartitionSpec as P

epsilon = 1e-06


def split_keys(keys, key_ids):
    key_rows = keys.shape[0]
    block_rows = math.gcd(key_rows, 512)
    key_blocks = keys.reshape(key_rows // block_rows, block_rows, keys.shape[1])
    id_blocks = key_ids.reshape(key_rows // block_rows, block_rows)
    return (key_blocks, id_blocks)


def block_scores(queries, members):
    width = queries.shape[1]
    return (
        lax.dot_general(
            queries, members, (((1,), (1,)), ((), ())), preferred_element_type=jnp.float32
        )
        / width
    )


def fold_rows(running, queries, query_ids, keys, key_ids):
    key_blocks, id_blocks = split_keys(keys, key_ids)

    def advance(carry, member):
        members, member_ids = member
        scores = block_scores(queries, members)
        scores = jnp.where(member_ids[None, :] < query_ids[:, None], scores, jnp.float32(-1.0))
        return (jnp.maximum(carry, jnp.max(scores, axis=1)), None)

    running, _ = lax.scan(advance, running, (key_blocks, id_blocks))
    return running


def on_device(embed, cluster):
    rows = embed.shape[0]
    width = embed.shape[1]
    shards = lax.axis_size("shard")
    groups = lax.axis_size("grp")
    capacity = 2 * rows // shards
    slots = shards * capacity
    sentinel = rows * shards * groups
    values = embed.astype(jnp.float32)
    mean_sq = jnp.mean(values * values, axis=1, keepdims=True)
    unit = (values * lax.rsqrt(mean_sq + epsilon)).astype(jnp.bfloat16)
    shard_pos = lax.axis_index("shard")
    group_pos = lax.axis_index("grp")
    base = (shard_pos * groups + group_pos) * rows
    global_ids = base + jnp.arange(rows, dtype=jnp.int32)
    owner = cluster[:, 0]
    onehot = (owner[:, None] == jnp.arange(shards, dtype=jnp.int32)[None, :]).astype(jnp.int32)
    within = jnp.sum((jnp.cumsum(onehot, axis=0) - onehot) * onehot, axis=1)
    slot_pos = owner * capacity + within
    slot_row = (
        jnp.full((slots,), rows, jnp.int32).at[slot_pos].set(jnp.arange(rows, dtype=jnp.int32))
    )
    unit_pad = jnp.concatenate([unit, jnp.zeros((1, width), jnp.bfloat16)], axis=0)
    ids_pad = jnp.concatenate([global_ids, jnp.full((1,), sentinel, jnp.int32)], axis=0)
    send_unit = unit_pad[slot_row].reshape(shards, capacity, width)
    send_ids = ids_pad[slot_row].reshape(shards, capacity)
    got_unit, got_ids = (
        lax.all_to_all(send_unit, "shard", split_axis=0, concat_axis=0, tiled=True),
        lax.all_to_all(send_ids, "shard", split_axis=0, concat_axis=0, tiled=True),
    )
    queries = got_unit.reshape(slots, width)
    query_ids = got_ids.reshape(slots)
    running = jnp.full((slots,), -1.0, jnp.float32)
    running = fold_rows(
        running,
        queries,
        query_ids,
        lax.all_gather(queries, "grp", axis=0, tiled=True),
        lax.all_gather(query_ids, "grp", axis=0, tiled=True),
    )
    homeward = lax.all_to_all(
        running.reshape(shards, capacity), "shard", split_axis=0, concat_axis=0, tiled=True
    )
    return homeward.reshape(slots)[slot_pos]


def solution(mesh):
    return jax.shard_map(
        on_device,
        mesh=mesh,
        in_specs=(P(("shard", "grp"), None), P(("shard", "grp"), None)),
        out_specs=P(("shard", "grp")),
        check_vma=False,
    )
```

profile of v0, /device:TPU:1, one launch (start us, length us, event | category | flops | bytes accessed | tf_op | source)
XLA Modules:
  0.0 186.2 jit_solution(15506365243214516289)
XLA Ops:
  6.5 0.8 fusion.9
  7.3 1.2 reduce-window.6
  8.8 0.8 fusion.8
  10.3 2.4 %scatter_custom_fusion = s32[1024]{0:T(1024)S(1)} fusion(s32[512]{0:T(512)S(1)} %bitcast.59, s32[512]{0:T(512)S(1)} %iota.15, s32[]{:T(128)} %constant.15.clone.1), kind=kCustom, calls=%fused_computation.30 | custom fusion | bytes 4100 | tf_op jit(solution)/shard_map/scatter | solution.py:62
  12.7 1.4 fusion.4
  14.4 4.0 %gather_fusion.1 = bf16[1024,768]{1,0:T(8,128)(2,1)S(1)} fusion(bf16[513,768]{1,0:T(8,128)(2,1)S(1)} %concatenate.7, s32[1024]{0:T(1024)S(1)} %fusion.10), kind=kCustom, calls=%fused_computation.1 | custom fusion | bytes 3149824 | tf_op jit(solution)/shard_map/gather | solution.py:66
  18.4 51.9 %all_to_all.26 = bf16[64,16,768]{2,1,0:T(8,128)(2,1)} all-to-all(bf16[64,16,768]{2,1,0:T(8,128)(2,1)S(1)} %bitcast.52), channel_id=1, replica_groups=mesh['shard'=64,'grp'=4] {'shard'}, dimensions={0} | all-to-all | bytes 3145728 | tf_op jit(solution)/shard_map/all_to_all | solution.py:69
  70.4 4.5 %gather_fusion = s32[1024]{0:T(1024)S(1)} fusion(s32[513]{0:T(1024)S(1)} %pad_add_fusion, s32[1024]{0:T(1024)S(1)} %fusion.10), kind=kCustom, calls=%fused_computation | custom fusion | bytes 12288 | tf_op jit(solution)/shard_map/gather | solution.py:67
  75.6 6.5 %all-to-all-start = ((s32[64,1,16]{2,1,0:T(1,128)}), s32[64,1,16]{2,1,0:T(1,128)S(1)}, u32[]{:S(2)}, u32[]{:S(2)}) async-start(s32[64,1,16]{2,1,0:T(1,128)} %bitcast.5), calls=%async_computation | async-start | bytes 65536 | tf_op jit(solution)/shard_map/all_to_all | solution.py:70
  82.1 9.4 %all-to-all-done = s32[64,1,16]{2,1,0:T(1,128)S(1)} async-done(((s32[64,1,16]{2,1,0:T(1,128)}), s32[64,1,16]{2,1,0:T(1,128)S(1)}, u32[]{:S(2)}, u32[]{:S(2)}) %all-to-all-start) | async-done | bytes 4128 | tf_op jit(solution)/shard_map/all_to_all | solution.py:70
  92.7 10.5 %all_gather.6 = s32[4096]{0:T(1024)S(1)} all-gather(s32[1024]{0:T(1024)S(1)} %reshape.55), channel_id=1, replica_groups=mesh['shard'=64,'grp'=4] {'grp'}, dimensions={0}, use_global_device_ids=true | all-gather | bytes 20480 | tf_op jit(solution)/shard_map/all_gather | solution.py:80
  103.2 32.9 %all-gather.2.cloned.1.call-done = bf16[4096,768]{1,0:T(8,128)(2,1)} async-done(((bf16[1024,768]{1,0:T(8,128)(2,1)}), bf16[4096,768]{1,0:T(8,128)(2,1)}) %all-gather.2.cloned.1.call-update) | async-done | bytes 6291472 | tf_op jit(solution)/shard_map/all_gather | solution.py:79
  136.1 17.7 %while.12 = (s32[]{:T(128)}, f32[1024]{0:T(1024)S(1)}, s32[8,512]{1,0:T(8,128)S(1)}, s32[64,16]{1,0:T(8,128)}, bf16[8,512,768]{2,1,0:T(8,128)(2,1)}, /*index=5*/...) while((s32[]{:T(128)}, f32[1024]{0:T(1024)S(1)}, ...), condition=%wide.wide.region_7.8_spmd.clone, body=%wide.wide.region_5.7_spmd.clone.sunk | while | flops 807404544 | bytes 2386539 | solution.py:38
  136.1 2.2 %fusion.22 = f32[1024]{0:T(1024)S(1)} fusion(bf16[1024,768]{1,0:T(8,128)(2,1)S(1)} %get-tuple-element.161, s32[1024]{0:T(1024)S(1)} %get-tuple-element.162, s32[512]{0:T(512)S(1)} %bitcast.55, bf16[8,512,768]{2,1,0:T(8,128)(2,1)} %get-tuple-element.160, s32[]{:T(128)} %get-tuple-element.147), kind=kOutput, calls=%fused_computation.5.clone.clone.1 | convolution fusion | flops 807402496 | bytes 2370048 | tf_op jit(solution)/shard_map/while/body/eval_jaxpr/dot_general | solution.py:22
  138.4 2.2 %fusion.22 = f32[1024]{0:T(1024)S(1)} fusion(bf16[1024,768]{1,0:T(8,128)(2,1)S(1)} %get-tuple-element.161, s32[1024]{0:T(1024)S(1)} %get-tuple-element.162, s32[512]{0:T(512)S(1)} %bitcast.55, bf16[8,512,768]{2,1,0:T(8,128)(2,1)} %get-tuple-element.160, s32[]{:T(128)} %get-tuple-element.147), kind=kOutput, calls=%fused_computation.5.clone.clone.1 | convolution fusion | flops 807402496 | bytes 2370048 | tf_op jit(solution)/shard_map/while/body/eval_jaxpr/dot_general | solution.py:22
  140.6 2.2 %fusion.22 = f32[1024]{0:T(1024)S(1)} fusion(bf16[1024,768]{1,0:T(8,128)(2,1)S(1)} %get-tuple-element.161, s32[1024]{0:T(1024)S(1)} %get-tuple-element.162, s32[512]{0:T(512)S(1)} %bitcast.55, bf16[8,512,768]{2,1,0:T(8,128)(2,1)} %get-tuple-element.160, s32[]{:T(128)} %get-tuple-element.147), kind=kOutput, calls=%fused_computation.5.clone.clone.1 | convolution fusion | flops 807402496 | bytes 2370048 | tf_op jit(solution)/shard_map/while/body/eval_jaxpr/dot_general | solution.py:22
  142.8 2.2 %fusion.22 = f32[1024]{0:T(1024)S(1)} fusion(bf16[1024,768]{1,0:T(8,128)(2,1)S(1)} %get-tuple-element.161, s32[1024]{0:T(1024)S(1)} %get-tuple-element.162, s32[512]{0:T(512)S(1)} %bitcast.55, bf16[8,512,768]{2,1,0:T(8,128)(2,1)} %get-tuple-element.160, s32[]{:T(128)} %get-tuple-element.147), kind=kOutput, calls=%fused_computation.5.clone.clone.1 | convolution fusion | flops 807402496 | bytes 2370048 | tf_op jit(solution)/shard_map/while/body/eval_jaxpr/dot_general | solution.py:22
  145.0 2.2 %fusion.22 = f32[1024]{0:T(1024)S(1)} fusion(bf16[1024,768]{1,0:T(8,128)(2,1)S(1)} %get-tuple-element.161, s32[1024]{0:T(1024)S(1)} %get-tuple-element.162, s32[512]{0:T(512)S(1)} %bitcast.55, bf16[8,512,768]{2,1,0:T(8,128)(2,1)} %get-tuple-element.160, s32[]{:T(128)} %get-tuple-element.147), kind=kOutput, calls=%fused_computation.5.clone.clone.1 | convolution fusion | flops 807402496 | bytes 2370048 | tf_op jit(solution)/shard_map/while/body/eval_jaxpr/dot_general | solution.py:22
  147.2 2.2 %fusion.22 = f32[1024]{0:T(1024)S(1)} fusion(bf16[1024,768]{1,0:T(8,128)(2,1)S(1)} %get-tuple-element.161, s32[1024]{0:T(1024)S(1)} %get-tuple-element.162, s32[512]{0:T(512)S(1)} %bitcast.55, bf16[8,512,768]{2,1,0:T(8,128)(2,1)} %get-tuple-element.160, s32[]{:T(128)} %get-tuple-element.147), kind=kOutput, calls=%fused_computation.5.clone.clone.1 | convolution fusion | flops 807402496 | bytes 2370048 | tf_op jit(solution)/shard_map/while/body/eval_jaxpr/dot_general | solution.py:22
  149.4 2.2 %fusion.22 = f32[1024]{0:T(1024)S(1)} fusion(bf16[1024,768]{1,0:T(8,128)(2,1)S(1)} %get-tuple-element.161, s32[1024]{0:T(1024)S(1)} %get-tuple-element.162, s32[512]{0:T(512)S(1)} %bitcast.55, bf16[8,512,768]{2,1,0:T(8,128)(2,1)} %get-tuple-element.160, s32[]{:T(128)} %get-tuple-element.147), kind=kOutput, calls=%fused_computation.5.clone.clone.1 | convolution fusion | flops 807402496 | bytes 2370048 | tf_op jit(solution)/shard_map/while/body/eval_jaxpr/dot_general | solution.py:22
  151.6 2.2 %fusion.22 = f32[1024]{0:T(1024)S(1)} fusion(bf16[1024,768]{1,0:T(8,128)(2,1)S(1)} %get-tuple-element.161, s32[1024]{0:T(1024)S(1)} %get-tuple-element.162, s32[512]{0:T(512)S(1)} %bitcast.55, bf16[8,512,768]{2,1,0:T(8,128)(2,1)} %get-tuple-element.160, s32[]{:T(128)} %get-tuple-element.147), kind=kOutput, calls=%fused_computation.5.clone.clone.1 | convolution fusion | flops 807402496 | bytes 2370048 | tf_op jit(solution)/shard_map/while/body/eval_jaxpr/dot_general | solution.py:22
  154.5 10.7 %all-to-all-start.2 = ((f32[64,1,16]{2,1,0:T(1,128)}), f32[64,1,16]{2,1,0:T(1,128)S(1)}, u32[]{:S(2)}, u32[]{:S(2)}) async-start(f32[64,1,16]{2,1,0:T(1,128)} %bitcast.10), calls=%async_computation.2 | async-start | bytes 65536 | tf_op jit(solution)/shard_map/all_to_all | solution.py:82
  165.2 9.4 %all-to-all-done.2 = f32[64,1,16]{2,1,0:T(1,128)S(1)} async-done(((f32[64,1,16]{2,1,0:T(1,128)}), f32[64,1,16]{2,1,0:T(1,128)S(1)}, u32[]{:S(2)}, u32[]{:S(2)}) %all-to-all-start.2) | async-done | bytes 4128 | tf_op jit(solution)/shard_map/all_to_all | solution.py:82
  175.9 3.4 %gather_fusion.2 = f32[512]{0:T(512)} fusion(f32[1024]{0:T(1024)S(1)} %reshape.60, s32[1024]{0:T(1024)S(1)} %pad_clamp_fusion), kind=kCustom, calls=%fused_computation.2 | custom fusion | bytes 6144 | tf_op jit(solution)/shard_map/gather | solution.py:85
  (47 shorter events, 5.3 us)
Async XLA Ops:
  6.5 7.6 %copy-start.1 = (bf16[512,768]{1,0:T(8,128)(2,1)S(1)}, bf16[512,768]{1,0:T(8,128)(2,1)}, u32[]{:S(2)}) copy-start(bf16[512,768]{1,0:T(8,128)(2,1)} %param.4) | copy-start | bytes 2359300
  6.5 129.6 %all-gather.2.cloned.1.call-start = ((), (), s32[]{:S(2)}) async-start(), calls=%async_computation.3 | async-start | bytes 7864320 | tf_op jit(solution)/shard_map/all_gather | solution.py:79
  70.4 65.8 %copy-start = (bf16[64,16,768]{2,1,0:T(8,128)(2,1)S(1)}, bf16[64,16,768]{2,1,0:T(8,128)(2,1)}, u32[]{:S(2)}) copy-start(bf16[64,16,768]{2,1,0:T(8,128)(2,1)} %all_to_all.26) | copy-start | bytes 4718596
  75.6 15.8 %all-to-all-start = ((s32[64,1,16]{2,1,0:T(1,128)}), s32[64,1,16]{2,1,0:T(1,128)S(1)}, u32[]{:S(2)}, u32[]{:S(2)}) async-start(s32[64,1,16]{2,1,0:T(1,128)} %bitcast.5), calls=%async_computation | async-start | bytes 65536 | tf_op jit(solution)/shard_map/all_to_all | solution.py:70
  91.4 44.7 %copy-start.2 = (s32[64,1,16]{2,1,0:T(1,128)}, s32[64,1,16]{2,1,0:T(1,128)S(1)}, u32[]{:S(2)}) copy-start(s32[64,1,16]{2,1,0:T(1,128)S(1)} %all-to-all-done) | copy-start | bytes 12292
  154.5 20.1 %all-to-all-start.2 = ((f32[64,1,16]{2,1,0:T(1,128)}), f32[64,1,16]{2,1,0:T(1,128)S(1)}, u32[]{:S(2)}, u32[]{:S(2)}) async-start(f32[64,1,16]{2,1,0:T(1,128)} %bitcast.10), calls=%async_computation.2 | async-start | bytes 65536 | tf_op jit(solution)/shard_map/all_to_all | solution.py:82
Sparse Core Ops, SparseCore 0:
  70.4 65.6 all-gather.1
where the time goes:
time: 187 us; the launch traced here: 186 us
  blocking collectives  62.4 us (33%)
  waiting for transfers between devices  51.7 us (28%)
  local copies, waits for them, and re-layouts  17.3 us (9%)
  matrix products  17.3 us (9%)
  starting transfers between devices  17.2 us (9%)
  between operations  13.5 us (7%)
  other arithmetic  6.49 us (3%)
    all_to_all x1, blocking collectives, on_device(): lax.all_to_all(send_unit, 'shard', split_axis=0, concat_axis=0, tiled=True)  51.9 us
    all_gather x1, waiting for transfers between devices, on_device(): lax.all_gather(queries, 'grp', axis=0, tiled=True)  32.9 us
    dot_general x8, matrix products, block_scores(): lax.dot_general(queries, members, (((1,), (1,)), ((), ())), preferred_ele...  17.3 us
    all_to_all x1, starting transfers between devices, on_device(): lax.all_to_all(running.reshape(shards, capacity), 'shard', split_axis=0,...  10.7 us
    all_gather x1, blocking collectives, on_device(): lax.all_gather(query_ids, 'grp', axis=0, tiled=True)  10.5 us
    all_to_all x1, waiting for transfers between devices, on_device(): lax.all_to_all(send_ids, 'shard', split_axis=0, concat_axis=0, tiled=True)  9.36 us
    all_to_all x1, waiting for transfers between devices, on_device(): lax.all_to_all(running.reshape(shards, capacity), 'shard', split_axis=0,...  9.36 us
    all_to_all x1, starting transfers between devices, on_device(): lax.all_to_all(send_ids, 'shard', split_axis=0, concat_axis=0, tiled=True)  6.46 us
  transfers between devices with their start and end apart: 3, of which 3 were waited for; matrix products, arithmetic and copies ran while one was open for 3% of the time, Pallas kernels for 0%

commit v1 on v0

v1 whole, which is shorter than its diff:
```python
import functools

import jax
import jax.numpy as jnp
from jax import lax
from jax.experimental import pallas as pl
from jax.experimental.pallas import tpu as pltpu
from jax.sharding import PartitionSpec as P

EPSILON = 1e-06
CORES = 2
CHIPS_X = 4
CAP = 16
LANES = 128
MARK = 64.0
LOW = -1e30
MESH = pl.DeviceIdType.MESH
F32 = jnp.float32
BF16 = jnp.bfloat16


def iota(shape, dim):
    return lax.broadcasted_iota(jnp.int32, shape, dim)


def kernel(
    nz, nx, ny, cap,
    cluster_ref, embed_ref, out_ref,
    unit, send, own, peer, best, reply, home,
    send_sem, recv_sem, swap_send_sem, swap_recv_sem, reply_send_sem, reply_recv_sem,
):
    rows, width = embed_ref.shape
    chips = nz * nx * ny
    owners = chips // 2
    half_y = ny // 2
    plane_owners = nx * half_y
    plane_rows = nx * ny * cap
    plane_slots = plane_owners * cap
    group = LANES // cap

    shard, y = lax.axis_index("shard"), lax.axis_index("grp")
    core = shard % CORES
    x = (shard // CORES) % nx
    z = shard // (CORES * nx)
    chip = (z * nx + x) * ny + y
    is_owner = (x + y + z) % 2 == 0
    my_cluster = (z * nx + x) * half_y + y // 2

    def device_of(chip_index):
        return ((chip_index // ny) * CORES + core, chip_index % ny)

    def owner_chip(zo, j):
        xo, h = j // half_y, j % half_y
        return (zo * nx + xo) * ny + 2 * h + (xo + zo) % 2

    peer_device = (shard + 1 - 2 * core, y)

    barrier = pltpu.get_barrier_semaphore()

    def greet(i, _):
        pl.semaphore_signal(
            barrier, inc=1, device_id=device_of((chip + 1 + i) % chips), device_id_type=MESH
        )
        return 0

    lax.fori_loop(0, chips - 1, greet, 0)
    pl.semaphore_signal(barrier, inc=1, device_id=peer_device, device_id_type=MESH)

    values = embed_ref[...].astype(F32)
    mean_sq = jnp.sum(values * values, axis=1, keepdims=True) / width
    unit[...] = (values * lax.rsqrt(mean_sq + EPSILON)).astype(BF16)
    cluster = cluster_ref[...]
    named = iota((owners, rows), 0) == cluster
    earlier = jnp.where(iota((rows, rows), 0) < iota((rows, rows), 1), 1.0, 0.0).astype(BF16)
    named_f32 = jnp.where(named, 1.0, 0.0)
    before = jnp.dot(named_f32.astype(BF16), earlier, preferred_element_type=F32)
    rank = jnp.sum(before * named_f32, axis=0, keepdims=True).astype(jnp.int32)
    slot = cluster * cap + rank

    pl.semaphore_wait(barrier, chips)

    offsets = [nz // 2]
    for step in range(nz // 2 - 1, 0, -1):
        offsets += [step, nz - step]
    offsets += [0]

    for offset in offsets:
        zo = (z + nz - offset) % nz
        first = pl.multiple_of(zo * plane_slots, plane_slots)
        chosen = jnp.where(iota((plane_slots, rows), 0) + first == slot, 1.0, 0.0)
        packed = jnp.dot(chosen.astype(BF16), unit[...], preferred_element_type=F32)
        filled = jnp.sum(chosen, axis=1, keepdims=True)
        send[pl.ds(first, plane_slots), :] = jnp.where(filled > 0.5, packed, MARK).astype(BF16)

        def post(j, _, zo=zo, first=first):
            target = owner_chip(zo, j)
            source = send.at[pl.ds(pl.multiple_of(first + j * cap, cap), cap)]
            landing = own.at[pl.ds(pl.multiple_of(chip * cap, cap), cap)]

            @pl.when(target == chip)
            def _():
                pltpu.make_async_copy(source, landing, recv_sem.at[z]).start()

            @pl.when(target != chip)
            def _():
                pltpu.make_async_remote_copy(
                    source, landing, send_sem, recv_sem.at[z],
                    device_id=device_of(target), device_id_type=MESH,
                ).start()

            return 0

        lax.fori_loop(0, plane_owners, post, 0)

    def plane(ref, index):
        return ref.at[pl.ds(pl.multiple_of(index * plane_rows, plane_rows), plane_rows)]

    def fold(keys, queries, query_plane, limit):
        found = keys[...]
        scores = lax.dot_general(
            found, queries[...], (((1,), (1,)), ((), ())), preferred_element_type=F32
        )
        bias = jnp.where(found[:, :LANES].astype(F32) > 32.0, LOW, 0.0)
        scores = scores + jnp.concatenate([bias] * (plane_rows // LANES), axis=1)
        if limit is not None:
            scores = jnp.where(limit, scores, LOW)
        row = pl.ds(query_plane, 1)
        best[row] = jnp.maximum(best[row], jnp.max(scores, axis=0, keepdims=True)[None])

    @pl.when(is_owner)
    def _():
        best[...] = jnp.full(best.shape, -float(width), F32)
        key_index = iota((plane_rows, plane_rows), 0)
        query_index = iota((plane_rows, plane_rows), 1)
        same_core = key_index < query_index
        per_x = ny * cap
        other_core = key_index // per_x < query_index // per_x + core

        def swap(zs):
            return pltpu.make_async_remote_copy(
                plane(own, zs), plane(peer, zs), swap_send_sem.at[zs], swap_recv_sem.at[zs],
                device_id=peer_device, device_id_type=MESH,
            )

        for step, offset in enumerate(offsets):
            zs = (z + offset) % nz
            pltpu.make_async_copy(plane(own, zs), plane(own, zs), recv_sem.at[zs]).wait()
            swap(zs).start()
            swap(zs).wait_recv()
            fold(plane(own, zs), plane(own, zs), zs, same_core)
            fold(plane(peer, zs), plane(own, zs), zs, other_core)

            def pair(t, _, zs=zs):
                zt = (z + offset_of(t)) % nz
                low, high = jnp.minimum(zs, zt), jnp.maximum(zs, zt)
                fold(plane(own, low), plane(own, high), high, None)
                fold(plane(peer, low), plane(own, high), high, None)
                return 0

            def offset_of(t):
                up = (t + 1) // 2
                return nz // 2 - up + (1 - t % 2) * 2 * up

            lax.fori_loop(0, step, pair, 0)

        result = jnp.maximum(best[...] / width, -1.0)
        pieces = plane_rows // LANES
        for piece in range(pieces):
            for zq in range(nz):
                reply[zq * pieces + piece] = result[zq][:, piece * LANES:(piece + 1) * LANES]

        def answer(i, _):
            target = (chip + 1 + i) % chips
            pltpu.make_async_remote_copy(
                reply.at[pl.ds(target // group, 1)], home.at[pl.ds(my_cluster, 1)],
                reply_send_sem, reply_recv_sem,
                device_id=device_of(target), device_id_type=MESH,
            ).start()
            return 0

        lax.fori_loop(0, chips - 1, answer, 0)
        pltpu.make_async_copy(
            reply.at[pl.ds(chip // group, 1)], home.at[pl.ds(my_cluster, 1)], reply_recv_sem
        ).start()

    waited = home.at[pl.ds(0, owners)]
    pltpu.make_async_copy(waited, waited, reply_recv_sem).wait()
    answers = home[...][:owners, 0, :]
    picked = lax.dot_general(
        answers, named_f32, (((0,), (0,)), ((), ())),
        preferred_element_type=F32, precision=lax.Precision.HIGHEST,
    )
    lane = (chip % group) * cap + rank
    out_ref[...] = jnp.sum(
        jnp.where(iota((LANES, rows), 0) == lane, picked, 0.0), axis=0, keepdims=True
    )

    @pl.when(is_owner)
    def _():
        sent = send.at[pl.ds(0, (owners - 1) * cap)]
        pltpu.make_async_copy(sent, sent, send_sem).wait()
        replied = home.at[pl.ds(0, chips - 1)]
        pltpu.make_async_copy(replied, replied, reply_send_sem).wait()
        for zs in range(nz):
            pltpu.make_async_copy(plane(own, zs), plane(own, zs), swap_send_sem.at[zs]).wait()

    @pl.when(jnp.logical_not(is_owner))
    def _():
        pltpu.make_async_copy(send, send, send_sem).wait()


def on_device(nz, nx, ny, cap, embed, cluster):
    rows, width = embed.shape
    chips = nz * nx * ny
    owners = chips // 2
    out = pl.pallas_call(
        functools.partial(kernel, nz, nx, ny, cap),
        out_shape=jax.ShapeDtypeStruct((1, rows), F32),
        in_specs=[pl.BlockSpec(memory_space=pltpu.VMEM)] * 2,
        out_specs=pl.BlockSpec(memory_space=pltpu.VMEM),
        scratch_shapes=[
            pltpu.VMEM((rows, width), BF16),
            pltpu.VMEM((owners * cap, width), BF16),
            pltpu.VMEM((chips * cap, width), BF16),
            pltpu.VMEM((chips * cap, width), BF16),
            pltpu.VMEM((nz, 1, nx * ny * cap), F32),
            pltpu.VMEM((chips * cap // LANES, 1, LANES), F32),
            pltpu.VMEM((chips, 1, LANES), F32),
            pltpu.SemaphoreType.DMA,
            pltpu.SemaphoreType.DMA((nz,)),
            pltpu.SemaphoreType.DMA((nz,)),
            pltpu.SemaphoreType.DMA((nz,)),
            pltpu.SemaphoreType.DMA,
            pltpu.SemaphoreType.DMA,
        ],
        compiler_params=pltpu.CompilerParams(
            collective_id=0, has_side_effects=True, vmem_limit_bytes=40 * 1024 * 1024
        ),
    )(cluster.reshape(1, rows), embed)
    return out.reshape(rows)


def solution(mesh, nx=CHIPS_X, cap=CAP):
    nz = mesh.shape["shard"] // (CORES * nx)
    ny = mesh.shape["grp"]
    return jax.shard_map(
        functools.partial(on_device, nz, nx, ny, cap),
        mesh=mesh,
        in_specs=(P(("shard", "grp"), None), P(("shard", "grp"), None)),
        out_specs=P(("shard", "grp")),
        check_vma=False,
    )
```

time: 187 us -> 86.4 us (0.46)
  Pallas kernels: 0 us -> 83.8 us
  blocking collectives: 62.4 us -> 0 us
  waiting for transfers between devices: 51.7 us -> 0 us
  matrix products: 17.3 us -> 0 us
  starting transfers between devices: 17.2 us -> 0 us
  local copies, waits for them, and re-layouts: 17.3 us -> 2.39 us
  between operations: 13.5 us -> 0.01 us
  other arithmetic: 6.49 us -> 0 us
    pallas_call x0 -> x1, Pallas kernels: none -> 83.8 us  [on_device(): pl.pallas_call(functools.partial(kernel, nz, nx, ny, cap), out_shape=jax....]
    all_to_all x1 -> x0, blocking collectives: 51.9 us -> none  [on_device(): lax.all_to_all(send_unit, 'shard', split_axis=0, concat_axis=0, tiled=True)]
    all_gather x1 -> x0, waiting for transfers between devices: 32.9 us -> none  [on_device(): lax.all_gather(queries, 'grp', axis=0, tiled=True)]
    all_to_all x2 -> x0, waiting for transfers between devices: 18.7 us -> none  [the longest x1 9.36 us: on_device(): lax.all_to_all(send_ids, 'shard', split_axis=0, concat_axis=0, tiled=True)]
    dot_general x8 -> x0, matrix products: 17.3 us -> none  [block_scores(): lax.dot_general(queries, members, (((1,), (1,)), ((), ())), preferred_ele...]
    all_to_all x2 -> x0, starting transfers between devices: 17.2 us -> none  [the longest x1 10.7 us: on_device(): lax.all_to_all(running.reshape(shards, capacity), 'shard', split_axis=0,...]
    gather x3 -> x0, local copies, waits for them, and re-layouts: 11.9 us -> none  [the longest x1 4.53 us: on_device(): send_ids = ids_pad[slot_row].reshape(shards, capacity)]
    all_gather x1 -> x0, blocking collectives: 10.5 us -> none  [on_device(): lax.all_gather(query_ids, 'grp', axis=0, tiled=True)]
  transfers between devices with their start and end apart: 3 -> 0, of which waited for: 3 -> 0; matrix products, arithmetic and copies ran while one was open for 3% -> 0% of each run, Pallas kernels for 0% -> 0%
where the time goes in v1:
time: 86.4 us; the launch traced here: 86.2 us
  Pallas kernels  83.8 us (97%)
  local copies, waits for them, and re-layouts  2.39 us (3%)
    pallas_call x1, Pallas kernels, on_device(): pl.pallas_call(functools.partial(kernel, nz, nx, ny, cap), out_shape=jax....  83.8 us
    unnamed x5, local copies, waits for them, and re-layouts  2.39 us

profile of v1, /device:TPU:1, one launch (start us, length us, event | category | flops | bytes accessed | tf_op | source)
XLA Modules:
  0.0 86.2 jit_solution(15873517266341320473)
XLA Ops:
  0.0 0.0 copy-start
  0.0 1.1 %copy-done = bf16[512,768]{1,0:T(8,128)(2,1)S(1)} copy-done((bf16[512,768]{1,0:T(8,128)(2,1)S(1)}, bf16[512,768]{1,0:T(8,128)(2,1)}, u32[]{:S(2)}) %copy-start) | copy-done | bytes 786456
  1.1 0.0 copy-start.1
  1.1 0.7 copy-done.1
  1.8 83.8 %shard_map.28 = f32[1,512]{1,0:T(1,128)S(1)} custom-call(s32[1,512]{1,0:T(1,128)S(1)} %bitcast.3, bf16[512,768]{1,0:T(8,128)(2,1)S(1)} %copy-done), custom_call_target="tpu_custom_call" | custom-call | tf_op jit(solution)/shard_map/pallas_call | solution.py:216
  85.7 0.6 copy.4
Async XLA Ops:
  0.0 1.1 %copy-start = (bf16[512,768]{1,0:T(8,128)(2,1)S(1)}, bf16[512,768]{1,0:T(8,128)(2,1)}, u32[]{:S(2)}) copy-start(bf16[512,768]{1,0:T(8,128)(2,1)} %embed_ref.1) | copy-start | bytes 2359300
  1.1 0.7 copy-start.1

commit v2 on v1

v2 whole, which is shorter than its diff:
```python
import functools

import jax
import jax.numpy as jnp
from jax import lax
from jax.experimental import pallas as pl
from jax.experimental.pallas import tpu as pltpu
from jax.sharding import PartitionSpec as P

EPSILON = 1e-06
CORES = 2
CHIPS_X = 4
CAP = 16
LANES = 128
MARK = 64.0
LOW = -1e30
MESH = pl.DeviceIdType.MESH
F32 = jnp.float32
BF16 = jnp.bfloat16


def iota(shape, dim):
    return lax.broadcasted_iota(jnp.int32, shape, dim)


def ring_messages(nz):
    far = nz // 2
    messages = [(d, h, u) for d in range(1, far) for h in range(1, d + 1) for u in range(2)]
    return messages + [(far, h, None) for h in range(1, far + 1)]


def kernel(
    nz, nx, ny, cap,
    cluster_ref, embed_ref, out_ref,
    embed, unit, send, ring, own, peer, best, reply, relay, home,
    embed_sem, ring_send, ring_recv, plane_send, plane_recv, swap_send, swap_recv,
    reply_send, relay_recv, home_recv,
):
    rows, width = embed.shape
    far = nz // 2
    places = nx * ny
    owners = nz * places // 2
    half_y = ny // 2
    plane_owners = nx * half_y
    half_owners = plane_owners // 2
    block = plane_owners * cap
    half = block // 2
    plane_rows = places * cap
    pieces = plane_rows // LANES
    group = LANES // cap
    number = {m: i for i, m in enumerate(ring_messages(nz))}

    shard, y = lax.axis_index("shard"), lax.axis_index("grp")
    core = lax.rem(shard, CORES)
    x = lax.rem(lax.div(shard, CORES), nx)
    z = lax.div(shard, CORES * nx)
    place = x * ny + y
    is_owner = lax.rem(x + y + z, 2) == 0
    z_at = [lax.rem(z + o, nz) for o in range(nz)]
    x_at = [lax.rem(x + o, nx) for o in range(nx)]
    y_at = [lax.rem(y + o, ny) for o in range(ny)]
    odd = [lax.rem(z, 2), lax.rem(z + 1, 2)]

    def device(zd, xd, yd):
        return ((zd * nx + xd) * CORES + core, yd)

    peer_device = (shard + 1 - 2 * core, y)
    others = [(ox, oy) for ox in range(nx) for oy in range(ny) if (ox, oy) != (0, 0)]

    fetch = pltpu.make_async_copy(embed_ref, embed, embed_sem)
    fetch.start()

    barrier = pltpu.get_barrier_semaphore()
    partners = [device(z_at[o], x, y) for o in range(1, nz)]
    partners += [device(z, x_at[ox], y_at[oy]) for ox, oy in others]
    partners += [peer_device]
    for partner in partners:
        pl.semaphore_signal(barrier, inc=1, device_id=partner, device_id_type=MESH)

    cluster = cluster_ref[...]
    named = jnp.where(iota((owners, rows), 0) == cluster, 1.0, 0.0)
    earlier = jnp.where(iota((rows, rows), 0) < iota((rows, rows), 1), 1.0, 0.0).astype(BF16)
    before = jnp.dot(named.astype(BF16), earlier, preferred_element_type=F32)
    rank = jnp.sum(before * named, axis=0, keepdims=True).astype(jnp.int32)
    slot = cluster * cap + rank
    fetch.wait()
    values = embed[...].astype(F32)
    mean_sq = jnp.sum(values * values, axis=1, keepdims=True) / width
    unit[...] = (values * lax.rsqrt(mean_sq + EPSILON)).astype(BF16)

    def pack(zo):
        first = pl.multiple_of(zo * block, block)
        chosen = jnp.where(iota((block, rows), 0) + first == slot, 1.0, 0.0)
        packed = jnp.dot(chosen.astype(BF16), unit[...], preferred_element_type=F32)
        filled = jnp.sum(chosen, axis=1, keepdims=True)
        send[pl.ds(first, block), :] = jnp.where(filled > 0.5, packed, MARK).astype(BF16)

    def half_of(direction, message):
        return direction if message[2] is None else message[2]

    def own_half(zo, u):
        return send.at[pl.ds(pl.multiple_of(zo * block + u * half, half), half)]

    def pass_on(direction, message, source):
        index = number[message]
        pltpu.make_async_remote_copy(
            source, ring.at[direction, index], ring_send, ring_recv.at[direction, index],
            device_id=device(z_at[1 if direction == 0 else nz - 1], x, y), device_id_type=MESH,
        ).start()

    def arrived(direction, message):
        index = number[message]
        buffer = ring.at[direction, index]
        pltpu.make_async_copy(buffer, buffer, ring_recv.at[direction, index]).wait()
        return buffer

    def spread(source, u, zs):
        landing = own.at[pl.ds(pl.multiple_of((zs * places + place) * cap, cap), cap)]
        for i in range(half_owners):
            j = u * half_owners + i
            xo, h = j // half_y, j % half_y
            yo = 2 * h + odd[xo % 2]
            mine = (x == xo) & (y == yo)
            part = source.at[pl.ds(i * cap, cap)]

            @pl.when(mine)
            def _():
                pltpu.make_async_copy(part, landing, plane_recv.at[zs]).start()

            @pl.when(jnp.logical_not(mine))
            def _():
                pltpu.make_async_remote_copy(
                    part, landing, plane_send, plane_recv.at[zs],
                    device_id=device(z, xo, yo), device_id_type=MESH,
                ).start()

    def plane(ref, index):
        return ref.at[pl.ds(pl.multiple_of(index * plane_rows, plane_rows), plane_rows)]

    def fold(keys, queries, query_plane, limit):
        found = keys[...]
        scores = lax.dot_general(
            found, queries[...], (((1,), (1,)), ((), ())), preferred_element_type=F32
        )
        bias = jnp.where(found[:, :LANES].astype(F32) > 32.0, LOW, 0.0)
        scores = scores + jnp.concatenate([bias] * pieces, axis=1)
        if limit is not None:
            scores = jnp.where(limit, scores, LOW)
        row = pl.ds(query_plane, 1)
        best[row] = jnp.maximum(best[row], jnp.max(scores, axis=0, keepdims=True)[None])

    def plane_of(t):
        return lax.rem(z + nz + (2 * lax.rem(t, 2) - 1) * lax.div(t + 1, 2), nz)

    def swap(zs):
        return pltpu.make_async_remote_copy(
            plane(own, zs), plane(peer, zs), swap_send.at[zs], swap_recv.at[zs],
            device_id=peer_device, device_id_type=MESH,
        )

    def score(first, last):
        @pl.when(is_owner)
        def _():
            def exchange(s, _):
                zs = plane_of(s)
                pltpu.make_async_copy(plane(own, zs), plane(own, zs), plane_recv.at[zs]).wait()
                swap(zs).start()
                return 0

            def take(s, _):
                swap(plane_of(s)).wait_recv()
                return 0

            def against(ref, shift):
                key = iota((plane_rows, plane_rows), 0)
                query = iota((plane_rows, plane_rows), 1)
                if shift is None:
                    limit = key < query
                else:
                    limit = lax.div(key, ny * cap) < lax.div(query, ny * cap) + shift

                def one(s, _):
                    zs = plane_of(s)
                    fold(plane(ref, zs), plane(own, zs), zs, limit)

                    def pair(t, _):
                        zt = plane_of(t)
                        low, high = jnp.minimum(zs, zt), jnp.maximum(zs, zt)
                        fold(plane(ref, low), plane(own, high), high, None)
                        return 0

                    return lax.fori_loop(0, s, pair, 0)

                lax.fori_loop(first, last + 1, one, 0)

            lax.fori_loop(first, last + 1, exchange, 0)
            against(own, None)
            lax.fori_loop(first, last + 1, take, 0)
            against(peer, core)

    both = ((0, 1), (1, -1))
    pl.semaphore_wait(barrier, len(partners))

    for d in range(1, far + 1):
        for direction, sign in both:
            zo = z_at[sign * d % nz]
            if d < far or direction == 0:
                pack(zo)
            for u in range(2) if d < far else (None,):
                message = (d, 1, u)
                pass_on(direction, message, own_half(zo, half_of(direction, message)))
    pack(z)
    for u in range(2):
        spread(own_half(z, u), u, z)
    best[...] = jnp.full(best.shape, -float(width), F32)

    def step(d, h):
        for u in range(2) if d < far else (None,):
            for direction, sign in both:
                buffer = arrived(direction, (d, h, u))
                if h < d:
                    pass_on(direction, (d, h + 1, u), buffer)
                else:
                    spread(buffer, half_of(direction, (d, h, u)), z_at[-sign * d % nz])

    for h in range(1, far + 1):
        for d in range(h, far + 1):
            step(d, h)
        if h < far - 1:
            score(0 if h == 1 else 2 * h - 1, 2 * h)
    if far > 1:
        score(2 * far - 3 if far > 2 else 0, 2 * far - 2)
    score(2 * far - 1 if far > 1 else 0, 2 * far - 1)

    @pl.when(is_owner)
    def _():
        result = jnp.maximum(best[...] / width, -1.0)
        for piece in range(pieces):
            reply[:, piece] = result[:, :, piece * LANES:(piece + 1) * LANES]
        slab = relay.at[:, lax.div(z, 2)]
        for o in range(1, nz):
            pltpu.make_async_remote_copy(
                reply.at[z_at[o]], slab, reply_send, relay_recv,
                device_id=device(z_at[o], x, y), device_id_type=MESH,
            ).start()
        pltpu.make_async_copy(reply.at[z], slab, relay_recv).start()

    pltpu.make_async_copy(relay, relay, relay_recv).wait()
    for ox, oy in others:
        target = x_at[ox] * ny + y_at[oy]
        pltpu.make_async_remote_copy(
            relay.at[lax.div(target, group)], home.at[place], reply_send, home_recv,
            device_id=device(z, x_at[ox], y_at[oy]), device_id_type=MESH,
        ).start()
    pltpu.make_async_copy(relay.at[lax.div(place, group)], home.at[place], home_recv).start()

    order = iota((owners, 1), 0)
    from_place, level = lax.div(order, far), lax.rem(order, far)
    from_x, from_y = lax.div(from_place, ny), lax.rem(from_place, ny)
    from_z = 2 * level + lax.rem(from_x + from_y, 2)
    held = (from_z * nx + from_x) * half_y + lax.div(from_y, 2)
    wanted = jnp.where(held == cluster, 1.0, 0.0)
    lane = lax.rem(place, group) * cap + rank
    pltpu.make_async_copy(home, home, home_recv).wait()
    answers = home[...].reshape(owners, LANES)
    picked = lax.dot_general(
        answers, wanted, (((0,), (0,)), ((), ())),
        preferred_element_type=F32, precision=lax.Precision.HIGHEST,
    )
    out_ref[...] = jnp.sum(
        jnp.where(iota((LANES, rows), 0) == lane, picked, 0.0), axis=0, keepdims=True
    )

    for direction, _ in both:
        sent = ring.at[direction]
        pltpu.make_async_copy(sent, sent, ring_send).wait()
    replied = home.at[pl.ds(0, places - 1)]
    pltpu.make_async_copy(replied, replied, reply_send).wait()

    @pl.when(is_owner)
    def _():
        passed = send.at[pl.ds(0, nz * (plane_owners - 1) * cap)]
        pltpu.make_async_copy(passed, passed, plane_send).wait()
        told = reply.at[pl.ds(0, nz - 1)]
        pltpu.make_async_copy(told, told, reply_send).wait()
        for zs in range(nz):
            pltpu.make_async_copy(plane(own, zs), plane(own, zs), swap_send.at[zs]).wait()

    @pl.when(jnp.logical_not(is_owner))
    def _():
        pltpu.make_async_copy(send, send, plane_send).wait()


def on_device(nz, nx, ny, cap, embed, cluster):
    rows, width = embed.shape
    places = nx * ny
    slots = nz * places * cap
    messages = len(ring_messages(nz))
    pieces = places * cap // LANES
    out = pl.pallas_call(
        functools.partial(kernel, nz, nx, ny, cap),
        out_shape=jax.ShapeDtypeStruct((1, rows), F32),
        in_specs=[
            pl.BlockSpec(memory_space=pltpu.VMEM),
            pl.BlockSpec(memory_space=pltpu.HBM),
        ],
        out_specs=pl.BlockSpec(memory_space=pltpu.VMEM),
        scratch_shapes=[
            pltpu.VMEM((rows, width), BF16),
            pltpu.VMEM((rows, width), BF16),
            pltpu.VMEM((slots // 2, width), BF16),
            pltpu.VMEM((2, messages, places * cap // 4, width), BF16),
            pltpu.VMEM((slots, width), BF16),
            pltpu.VMEM((slots, width), BF16),
            pltpu.VMEM((nz, 1, places * cap), F32),
            pltpu.VMEM((nz, pieces, 1, LANES), F32),
            pltpu.VMEM((pieces, nz // 2, 1, LANES), F32),
            pltpu.VMEM((places, nz // 2, 1, LANES), F32),
            pltpu.SemaphoreType.DMA,
            pltpu.SemaphoreType.DMA,
            pltpu.SemaphoreType.DMA((2, messages)),
            pltpu.SemaphoreType.DMA,
            pltpu.SemaphoreType.DMA((nz,)),
            pltpu.SemaphoreType.DMA((nz,)),
            pltpu.SemaphoreType.DMA((nz,)),
            pltpu.SemaphoreType.DMA,
            pltpu.SemaphoreType.DMA,
            pltpu.SemaphoreType.DMA,
        ],
        compiler_params=pltpu.CompilerParams(
            collective_id=0, has_side_effects=True, vmem_limit_bytes=40 * 1024 * 1024
        ),
    )(cluster.reshape(1, rows), embed)
    return out.reshape(rows)


def solution(mesh, nx=CHIPS_X, cap=CAP):
    nz = mesh.shape["shard"] // (CORES * nx)
    ny = mesh.shape["grp"]
    return jax.shard_map(
        functools.partial(on_device, nz, nx, ny, cap),
        mesh=mesh,
        in_specs=(P(("shard", "grp"), None), P(("shard", "grp"), None)),
        out_specs=P(("shard", "grp")),
        check_vma=False,
    )
```

time: 86.4 us -> 81.6 us (0.944)
  Pallas kernels: 83.8 us -> 78.2 us
    pallas_call x1, Pallas kernels: 83.8 us -> 78.2 us  [on_device(): pl.pallas_call(functools.partial(kernel, nz, nx, ny, cap), out_shape=jax....]
where the time goes in v2:
time: 81.6 us; the launch traced here: 80.6 us
  Pallas kernels  78.2 us (96%)
  local copies, waits for them, and re-layouts  2.39 us (3%)
    pallas_call x1, Pallas kernels, on_device(): pl.pallas_call(functools.partial(kernel, nz, nx, ny, cap), out_shape=jax....  78.2 us
    unnamed x5, local copies, waits for them, and re-layouts  2.39 us

profile of v2, /device:TPU:1, one launch (start us, length us, event | category | flops | bytes accessed | tf_op | source)
XLA Modules:
  0.0 80.6 jit_solution(14942087784623348282)
XLA Ops:
  0.0 0.0 copy-start
  0.0 1.1 %copy-done = bf16[512,768]{1,0:T(8,128)(2,1)S(1)} copy-done((bf16[512,768]{1,0:T(8,128)(2,1)S(1)}, bf16[512,768]{1,0:T(8,128)(2,1)}, u32[]{:S(2)}) %copy-start) | copy-done | bytes 786456
  1.1 0.0 copy-start.1
  1.1 0.7 copy-done.1
  1.8 78.2 %shard_map.28 = f32[1,512]{1,0:T(1,128)S(1)} custom-call(s32[1,512]{1,0:T(1,128)S(1)} %bitcast.3, bf16[512,768]{1,0:T(8,128)(2,1)S(1)} %copy-done), custom_call_target="tpu_custom_call" | custom-call | tf_op jit(solution)/shard_map/pallas_call | solution.py:300
  80.0 0.6 copy.4
Async XLA Ops:
  0.0 1.1 %copy-start = (bf16[512,768]{1,0:T(8,128)(2,1)S(1)}, bf16[512,768]{1,0:T(8,128)(2,1)}, u32[]{:S(2)}) copy-start(bf16[512,768]{1,0:T(8,128)(2,1)} %embed_ref.1) | copy-start | bytes 2359300
  1.1 0.7 copy-start.1

commit v3 on v2

--- a/solution.py
+++ b/solution.py
@@ -146,11 +146,11 @@
         scores = scores + jnp.concatenate([bias] * pieces, axis=1)
         if limit is not None:
             scores = jnp.where(limit, scores, LOW)
-        row = pl.ds(query_plane, 1)
-        best[row] = jnp.maximum(best[row], jnp.max(scores, axis=0, keepdims=True)[None])
+        top = jnp.max(scores.reshape(plane_rows // 8, 8, plane_rows), axis=0)
+        best[query_plane] = jnp.maximum(best[query_plane], top)
 
     def plane_of(t):
-        return lax.rem(z + nz + (2 * lax.rem(t, 2) - 1) * lax.div(t + 1, 2), nz)
+        return z_at[(2 * (t % 2) - 1) * ((t + 1) // 2) % nz]
 
     def swap(zs):
         return pltpu.make_async_remote_copy(
@@ -161,15 +161,7 @@
     def score(first, last):
         @pl.when(is_owner)
         def _():
-            def exchange(s, _):
-                zs = plane_of(s)
-                pltpu.make_async_copy(plane(own, zs), plane(own, zs), plane_recv.at[zs]).wait()
-                swap(zs).start()
-                return 0
-
-            def take(s, _):
-                swap(plane_of(s)).wait_recv()
-                return 0
+            steps = [plane_of(s) for s in range(last + 1)]
 
             def against(ref, shift):
                 key = iota((plane_rows, plane_rows), 0)
@@ -178,24 +170,19 @@
                     limit = key < query
                 else:
                     limit = lax.div(key, ny * cap) < lax.div(query, ny * cap) + shift
-
-                def one(s, _):
-                    zs = plane_of(s)
+                for s in range(first, last + 1):
+                    zs = steps[s]
                     fold(plane(ref, zs), plane(own, zs), zs, limit)
-
-                    def pair(t, _):
-                        zt = plane_of(t)
+                    for zt in steps[:s]:
                         low, high = jnp.minimum(zs, zt), jnp.maximum(zs, zt)
                         fold(plane(ref, low), plane(own, high), high, None)
-                        return 0
-
-                    return lax.fori_loop(0, s, pair, 0)
-
-                lax.fori_loop(first, last + 1, one, 0)
-
-            lax.fori_loop(first, last + 1, exchange, 0)
+
+            for zs in steps[first:]:
+                pltpu.make_async_copy(plane(own, zs), plane(own, zs), plane_recv.at[zs]).wait()
+                swap(zs).start()
             against(own, None)
-            lax.fori_loop(first, last + 1, take, 0)
+            for zs in steps[first:]:
+                swap(zs).wait_recv()
             against(peer, core)
 
     both = ((0, 1), (1, -1))
@@ -226,15 +213,17 @@
     for h in range(1, far + 1):
         for d in range(h, far + 1):
             step(d, h)
-        if h < far - 1:
-            score(0 if h == 1 else 2 * h - 1, 2 * h)
+        if h == far - 2:
+            score(0, 2 * h)
+    near = 2 * far - 4
     if far > 1:
-        score(2 * far - 3 if far > 2 else 0, 2 * far - 2)
+        score(near + 1 if far > 2 else 0, near + 2)
     score(2 * far - 1 if far > 1 else 0, 2 * far - 1)
 
     @pl.when(is_owner)
     def _():
-        result = jnp.maximum(best[...] / width, -1.0)
+        result = jnp.max(best[...], axis=1, keepdims=True)
+        result = jnp.maximum(result / width, -1.0)
         for piece in range(pieces):
             reply[:, piece] = result[:, :, piece * LANES:(piece + 1) * LANES]
         slab = relay.at[:, lax.div(z, 2)]
@@ -312,7 +301,7 @@
             pltpu.VMEM((2, messages, places * cap // 4, width), BF16),
             pltpu.VMEM((slots, width), BF16),
             pltpu.VMEM((slots, width), BF16),
-            pltpu.VMEM((nz, 1, places * cap), F32),
+            pltpu.VMEM((nz, 8, places * cap), F32),
             pltpu.VMEM((nz, pieces, 1, LANES), F32),
             pltpu.VMEM((pieces, nz // 2, 1, LANES), F32),
             pltpu.VMEM((places, nz // 2, 1, LANES), F32),
@@ -328,7 +317,7 @@
             pltpu.SemaphoreType.DMA,
         ],
         compiler_params=pltpu.CompilerParams(
-            collective_id=0, has_side_effects=True, vmem_limit_bytes=40 * 1024 * 1024
+            collective_id=0, has_side_effects=True, vmem_limit_bytes=(64 * 1024 - 256) * 1024
         ),
     )(cluster.reshape(1, rows), embed)
     return out.reshape(rows)

time: 81.6 us -> 73.9 us (0.906)
  Pallas kernels: 78.2 us -> 71.7 us
  local copies, waits for them, and re-layouts: 2.39 us -> 1.26 us
    pallas_call x1, Pallas kernels: 78.2 us -> 71.7 us  [on_device(): pl.pallas_call(functools.partial(kernel, nz, nx, ny, cap), out_shape=jax....]
    unnamed x5 -> x1, local copies, waits for them, and re-layouts: 2.39 us -> 1.26 us
where the time goes in v3:
time: 73.9 us; the launch traced here: 72.9 us
  Pallas kernels  71.7 us (97%)
  local copies, waits for them, and re-layouts  1.26 us (2%)
    pallas_call x1, Pallas kernels, on_device(): pl.pallas_call(functools.partial(kernel, nz, nx, ny, cap), out_shape=jax....  71.7 us

profile of v3, /device:TPU:1, one launch (start us, length us, event | category | flops | bytes accessed | tf_op | source)
XLA Modules:
  0.0 72.9 jit_solution(6774304618499301744)
XLA Ops:
  0.0 71.7 %shard_map.28 = f32[1,512]{1,0:T(1,128)} custom-call(s32[1,512]{1,0:T(1,128)} %bitcast.3, bf16[512,768]{1,0:T(8,128)(2,1)} %embed_ref.1), custom_call_target="tpu_custom_call" | custom-call | tf_op jit(solution)/shard_map/pallas_call | solution.py:289
  71.7 1.3 %copy.4 = f32[512]{0:T(512)} copy(f32[512]{0:T(512)} %bitcast.2) | data formatting | bytes 4096

commit v4 on v3

v4 whole, which is shorter than its diff:
```python
import functools

import jax
import jax.numpy as jnp
from jax import lax
from jax.experimental import pallas as pl
from jax.experimental.pallas import tpu as pltpu
from jax.sharding import PartitionSpec as P

EPSILON = 1e-06
CORES = 2
CAP = 16
LANES = 128
MARK = 64.0
LOW = -1e30
MESH = pl.DeviceIdType.MESH
F32 = jnp.float32
BF16 = jnp.bfloat16


def iota(shape, dim):
    return lax.broadcasted_iota(jnp.int32, shape, dim)


def wait_for(ref, semaphore):
    pltpu.make_async_copy(ref, ref, semaphore).wait()


RING_ORDER = {
    2: ((2, 1, None), (1, 1, 0), (2, 2, None), (1, 1, 1)),
    4: (
        (1, 1, 0), (1, 1, 1), (2, 1, 0), (2, 1, 1), (2, 2, 0), (3, 1, 0), (2, 2, 1), (3, 2, 0),
        (4, 1, None), (3, 1, 1), (4, 2, None), (3, 3, 0), (3, 2, 1), (4, 3, None), (3, 3, 1),
        (4, 4, None),
    ),
}
AHEAD = 4
SPREAD_HERE = 5
OWNER_WORK = {
    2: ((4, "meet", 0, 2), (4, "own", 0, 2), (4, "peer", 0, 2)),
    4: (
        (8, "meet", 0, 2), (9, "own", 0, 2), (10, "peer", 0, 2),
        (11, "meet", 3, 4), (12, "own", 3, 4), (14, "peer", 3, 4),
        (16, "meet", 5, 6), (16, "own", 5, 6),
    ),
}


def kernel(
    nz, side, cap,
    cluster_ref, embed_ref, out_ref,
    cluster_rows, embed, unit, send, lined, ring, own, peer, best, reply, relay, home,
    fetch_sem, line_send, line_recv, ring_send, ring_recv, plane_send, plane_recv,
    swap_send, swap_recv, reply_send, relay_recv, home_recv,
):
    rows, width = embed.shape
    far = nz // 2
    places = side * side
    per_line = side // 2
    owners = nz * side * per_line
    block = side * per_line * cap
    plane_rows = places * cap
    pieces = plane_rows // LANES
    group = LANES // cap
    order = RING_ORDER[far]

    shard, y = lax.axis_index("shard"), lax.axis_index("grp")
    core = lax.rem(shard, CORES)
    x = lax.rem(lax.div(shard, CORES), side)
    z = lax.div(shard, CORES * side)
    a, b = x + core * (y - x), y + core * (x - y)
    place = b * side + a
    is_owner = lax.rem(x + y + z, 2) == 0
    z_at = [lax.rem(z + o, nz) for o in range(nz)]
    a_at = [lax.rem(a + o, side) for o in range(side)]
    b_at = [lax.rem(b + o, side) for o in range(side)]

    def device(zd, ad, bd):
        xd, yd = ad + core * (bd - ad), bd + core * (ad - bd)
        return ((zd * side + xd) * CORES + core, yd)

    peer_device = (shard + 1 - 2 * core, y)
    others = [(oa, ob) for oa in range(side) for ob in range(side) if (oa, ob) != (0, 0)]

    fetch_cluster = pltpu.make_async_copy(cluster_ref, cluster_rows, fetch_sem.at[0])
    fetch_embed = pltpu.make_async_copy(embed_ref, embed, fetch_sem.at[1])
    fetch_cluster.start()
    fetch_embed.start()

    barrier = pltpu.get_barrier_semaphore()
    partners = [device(z_at[o], a, b) for o in range(1, nz)]
    partners += [device(z, a_at[oa], b_at[ob]) for oa, ob in others]
    partners += [peer_device]
    for partner in partners:
        pl.semaphore_signal(barrier, inc=1, device_id=partner, device_id_type=MESH)

    fetch_cluster.wait()
    cluster = cluster_rows[...]
    to_z = lax.div(cluster, side * per_line)
    to_x = lax.rem(lax.div(cluster, per_line), side)
    to_y = 2 * lax.rem(cluster, per_line) + lax.rem(to_x + to_z, 2)
    to_a, to_b = to_x + core * (to_y - to_x), to_y + core * (to_x - to_y)
    owner = (to_z * side + to_a) * per_line + lax.div(to_b, 2)
    named = jnp.where(iota((owners, rows), 0) == owner, 1.0, 0.0)
    earlier = jnp.where(iota((rows, rows), 0) < iota((rows, rows), 1), 1.0, 0.0).astype(BF16)
    before = jnp.dot(named.astype(BF16), earlier, preferred_element_type=F32)
    rank = jnp.sum(before * named, axis=0, keepdims=True).astype(jnp.int32)
    slot = owner * cap + rank

    fetch_embed.wait()
    values = embed[...].astype(F32)
    mean_sq = jnp.sum(values * values, axis=1, keepdims=True) / width
    unit[...] = (values * lax.rsqrt(mean_sq + EPSILON)).astype(BF16)

    def pack(zo):
        chosen = jnp.where(iota((block, rows), 0) + zo * block == slot, 1.0, 0.0)
        packed = jnp.dot(chosen.astype(BF16), unit[...], preferred_element_type=F32)
        filled = jnp.sum(chosen, axis=1, keepdims=True)
        packed = jnp.where(filled > 0.5, packed, MARK).astype(BF16)
        send[pl.ds(zo * side, side)] = packed.reshape(side, per_line, cap, width)

    def line_up(zo):
        pack(zo)
        for o in range(1, side):
            pltpu.make_async_remote_copy(
                send.at[zo * side + a_at[o]], lined.at[zo, a], line_send, line_recv.at[zo],
                device_id=device(z, a_at[o], b), device_id_type=MESH,
            ).start()
        pltpu.make_async_copy(
            send.at[zo * side + a], lined.at[zo, a], line_recv.at[zo]
        ).start()

    def pass_on(direction, index):
        d, h, u = order[index]
        if h == 1:
            zo = z_at[d if direction == 0 else nz - d]
            first = per_line * (direction if u is None else u)
            if d == 1:
                source = send.at[pl.ds(zo * side + first, per_line)]
            else:
                source = lined.at[zo, pl.ds(first, per_line)]
        else:
            source = ring.at[direction, order.index((d, h - 1, u))]
        pltpu.make_async_remote_copy(
            source, ring.at[direction, index], ring_send, ring_recv.at[direction, index],
            device_id=device(z_at[1 if direction == 0 else nz - 1], a, b), device_id_type=MESH,
        ).start()

    def spread(source, first, zs):
        landing = own.at[pl.ds((zs * side + b) * side + first, source.shape[0])]
        for g in range(per_line):
            owner_b = 2 * g + lax.rem(a + z, 2)
            part = source.at[:, g]

            @pl.when(b == owner_b)
            def _():
                pltpu.make_async_copy(part, landing, plane_recv.at[zs]).start()

            @pl.when(b != owner_b)
            def _():
                pltpu.make_async_remote_copy(
                    part, landing, plane_send, plane_recv.at[zs],
                    device_id=device(z, a, owner_b), device_id_type=MESH,
                ).start()

    def spread_near(source, first, zs):
        landing = own.at[(zs * side + b) * side + a]
        for i in range(per_line):
            for g in range(per_line):
                owner_a = first + i
                owner_b = 2 * g + lax.rem(owner_a + z, 2)
                mine = (a == owner_a) & (b == owner_b)

                @pl.when(mine)
                def _():
                    pltpu.make_async_copy(source.at[i, g], landing, plane_recv.at[zs]).start()

                @pl.when(jnp.logical_not(mine))
                def _():
                    pltpu.make_async_remote_copy(
                        source.at[i, g], landing, plane_send, plane_recv.at[zs],
                        device_id=device(z, owner_a, owner_b), device_id_type=MESH,
                    ).start()

    def plane(ref, index):
        return ref.at[pl.ds(index * places, places)]

    def fold(keys, queries, query_plane, limit):
        found = keys[...].reshape(plane_rows, width)
        asked = queries[...].reshape(plane_rows, width)
        scores = lax.dot_general(
            found, asked, (((1,), (1,)), ((), ())), preferred_element_type=F32
        )
        bias = jnp.where(found[:, :LANES].astype(F32) > 32.0, LOW, 0.0)
        scores = scores + jnp.concatenate([bias] * pieces, axis=1)
        if limit is not None:
            scores = jnp.where(limit, scores, LOW)
        top = jnp.max(scores.reshape(plane_rows // 8, 8, plane_rows), axis=0)
        best[query_plane] = jnp.maximum(best[query_plane], top)

    def plane_of(t):
        return z_at[(2 * (t % 2) - 1) * ((t + 1) // 2) % nz]

    def file_order(index, from_core):
        at_b, at_a = lax.div(index, side * cap), lax.rem(lax.div(index, cap), side)
        at_x, at_y = at_a + from_core * (at_b - at_a), at_b + from_core * (at_a - at_b)
        return ((at_x * CORES + from_core) * side + at_y) * cap + lax.rem(index, cap)

    def swap(zs):
        return pltpu.make_async_remote_copy(
            plane(own, zs), plane(peer, zs), swap_send.at[zs], swap_recv.at[zs],
            device_id=peer_device, device_id_type=MESH,
        )

    steps = [plane_of(t) for t in range(nz)]

    def against(ref, from_core, first, last):
        key = file_order(iota((plane_rows, 1), 0), from_core)
        query = file_order(iota((1, plane_rows), 1), core)
        limit = key < query
        for s in range(first, last + 1):
            zs = steps[s]
            fold(plane(ref, zs), plane(own, zs), zs, limit)
            for zt in steps[:s]:
                low, high = jnp.minimum(zs, zt), jnp.maximum(zs, zt)
                fold(plane(ref, low), plane(own, high), high, None)

    def work(what, first, last):
        @pl.when(is_owner)
        def _():
            if what == "meet":
                for zs in steps[first:last + 1]:
                    wait_for(plane(own, zs), plane_recv.at[zs])
                    swap(zs).start()
            elif what == "own":
                against(own, core, first, last)
            else:
                for zs in steps[first:last + 1]:
                    wait_for(plane(peer, zs), swap_recv.at[zs])
                against(peer, 1 - core, first, last)

    ready = [0 if h == 1 else order.index((d, h - 1, u)) + 1 for d, h, u in order]
    begins = [max(0, i + 1 - AHEAD, r) for i, r in enumerate(ready)]
    for i in range(1, len(begins)):
        begins[i] = max(begins[i], begins[i - 1])
    waited = set()
    sent_first = [order.index((1, 1, u)) for u in range(2 if far > 2 else 1)]

    def line_ready(offset):
        if offset not in waited:
            waited.add(offset)
            wait_for(lined.at[z_at[offset]], line_recv.at[z_at[offset]])

    def send_after(count):
        for index, (d, h, _) in enumerate(order):
            if begins[index] == count and index not in sent_first:
                for direction in range(2):
                    if h == 1 and d > 1:
                        line_ready(d if direction == 0 else nz - d)
                    pass_on(direction, index)

    pl.semaphore_wait(barrier, len(partners))
    for offset in (1, nz - 1):
        pack(z_at[offset])
        for index in range(2 if far > 2 else 1):
            pass_on(0 if offset == 1 else 1, order.index((1, 1, index)))
    for offset in [sign * d % nz for d in range(2, far) for sign in (1, -1)] + [far, 0]:
        line_up(z_at[offset])
    send_after(0)
    best[...] = jnp.full(best.shape, -float(width), F32)
    for count, message in enumerate(order, 1):
        d, h, u = message
        for direction in range(2):
            buffer = ring.at[direction, count - 1]
            wait_for(buffer, ring_recv.at[direction, count - 1])
            if h == d:
                zs = z_at[nz - d if direction == 0 else d]
                first = per_line * (direction if u is None else u)
                (spread_near if d == 1 else spread)(buffer, first, zs)
        send_after(count)
        if count == min(SPREAD_HERE, len(order)):
            line_ready(0)
            spread(lined.at[z], 0, z)
        for after, what, first, last in OWNER_WORK[far]:
            if after == count:
                work(what, first, last)
    last = nz - 1
    work("meet", last, last)
    if far > 2:
        work("peer", last - 2, last - 1)
    work("own", last, last)
    work("peer", last, last)

    @pl.when(is_owner)
    def _():
        result = jnp.max(best[...], axis=1, keepdims=True)
        result = jnp.maximum(result / width, -1.0)
        for piece in range(pieces):
            reply[:, piece] = result[:, :, piece * LANES:(piece + 1) * LANES]
        slab = relay.at[:, lax.div(z, 2)]
        for o in range(1, nz):
            pltpu.make_async_remote_copy(
                reply.at[z_at[o]], slab, reply_send, relay_recv,
                device_id=device(z_at[o], a, b), device_id_type=MESH,
            ).start()
        pltpu.make_async_copy(reply.at[z], slab, relay_recv).start()

    wait_for(relay, relay_recv)
    for oa, ob in others:
        target = b_at[ob] * side + a_at[oa]
        pltpu.make_async_remote_copy(
            relay.at[lax.div(target, group)], home.at[place], reply_send, home_recv,
            device_id=device(z, a_at[oa], b_at[ob]), device_id_type=MESH,
        ).start()
    pltpu.make_async_copy(relay.at[lax.div(place, group)], home.at[place], home_recv).start()

    entry = iota((owners, 1), 0)
    from_place, level = lax.div(entry, far), lax.rem(entry, far)
    from_b, from_a = lax.div(from_place, side), lax.rem(from_place, side)
    from_z = 2 * level + lax.rem(from_a + from_b, 2)
    held = (from_z * side + from_a) * per_line + lax.div(from_b, 2)
    wanted = jnp.where(held == owner, 1.0, 0.0)
    lane = lax.rem(place, group) * cap + rank
    wait_for(home, home_recv)
    answers = home[...].reshape(owners, LANES)
    picked = lax.dot_general(
        answers, wanted, (((0,), (0,)), ((), ())),
        preferred_element_type=F32, precision=lax.Precision.HIGHEST,
    )
    out_ref[...] = jnp.sum(
        jnp.where(iota((LANES, rows), 0) == lane, picked, 0.0), axis=0, keepdims=True
    )

    lines = send.at[pl.ds(0, (nz - 2) * (side - 1))]
    wait_for(lines, line_send)
    for direction in range(2):
        sent = ring.at[direction]
        wait_for(sent, ring_send)
    replied = home.at[pl.ds(0, places - 1)]
    wait_for(replied, reply_send)

    @pl.when(is_owner)
    def _():
        passed = 2 * (side * per_line - 1) + (nz - 2) * side * (per_line - 1)
        wait_for(own.at[pl.ds(0, passed)], plane_send)
        told = reply.at[pl.ds(0, nz - 1)]
        wait_for(told, reply_send)
        for zs in range(nz):
            wait_for(plane(own, zs), swap_send.at[zs])

    @pl.when(jnp.logical_not(is_owner))
    def _():
        wait_for(own.at[pl.ds(0, nz * side * per_line)], plane_send)


def on_device(nz, side, cap, embed, cluster):
    rows, width = embed.shape
    places = side * side
    per_line = side // 2
    messages = len(RING_ORDER[nz // 2])
    pieces = places * cap // LANES
    out = pl.pallas_call(
        functools.partial(kernel, nz, side, cap),
        out_shape=jax.ShapeDtypeStruct((1, rows), F32),
        in_specs=[pl.BlockSpec(memory_space=pltpu.HBM)] * 2,
        out_specs=pl.BlockSpec(memory_space=pltpu.VMEM),
        scratch_shapes=[
            pltpu.VMEM((1, rows), jnp.int32),
            pltpu.VMEM((rows, width), BF16),
            pltpu.VMEM((rows, width), BF16),
            pltpu.VMEM((nz * side, per_line, cap, width), BF16),
            pltpu.VMEM((nz, side, per_line, cap, width), BF16),
            pltpu.VMEM((2, messages, per_line, per_line, cap, width), BF16),
            pltpu.VMEM((nz * places, cap, width), BF16),
            pltpu.VMEM((nz * places, cap, width), BF16),
            pltpu.VMEM((nz, 8, places * cap), F32),
            pltpu.VMEM((nz, pieces, 1, LANES), F32),
            pltpu.VMEM((pieces, nz // 2, 1, LANES), F32),
            pltpu.VMEM((places, nz // 2, 1, LANES), F32),
            pltpu.SemaphoreType.DMA((2,)),
            pltpu.SemaphoreType.DMA,
            pltpu.SemaphoreType.DMA((nz,)),
            pltpu.SemaphoreType.DMA,
            pltpu.SemaphoreType.DMA((2, messages)),
            pltpu.SemaphoreType.DMA,
            pltpu.SemaphoreType.DMA((nz,)),
            pltpu.SemaphoreType.DMA((nz,)),
            pltpu.SemaphoreType.DMA((nz,)),
            pltpu.SemaphoreType.DMA,
            pltpu.SemaphoreType.DMA,
            pltpu.SemaphoreType.DMA,
        ],
        compiler_params=pltpu.CompilerParams(
            collective_id=0, has_side_effects=True, vmem_limit_bytes=(64 * 1024 - 512) * 1024
        ),
    )(cluster.reshape(1, rows), embed)
    return out.reshape(rows)


def solution(mesh, cap=CAP):
    side = mesh.shape["grp"]
    nz = mesh.shape["shard"] // (CORES * side)
    return jax.shard_map(
        functools.partial(on_device, nz, side, cap),
        mesh=mesh,
        in_specs=(P(("shard", "grp"), None), P(("shard", "grp"), None)),
        out_specs=P(("shard", "grp")),
        check_vma=False,
    )
```

time: 73.9 us -> 70.4 us (0.953); the launches traced: 72.9 us -> 70.3 us
  Pallas kernels: 71.7 us -> 69.1 us
    pallas_call x1, Pallas kernels: 71.7 us -> 69.1 us  [on_device(): pl.pallas_call(functools.partial(kernel, nz, side, cap), out_shape=jax.Sh...]
where the time goes in v4:
time: 70.4 us; the launch traced here: 70.3 us
  Pallas kernels  69.1 us (98%)
  local copies, waits for them, and re-layouts  1.26 us (2%)
    pallas_call x1, Pallas kernels, on_device(): pl.pallas_call(functools.partial(kernel, nz, side, cap), out_shape=jax.Sh...  69.1 us

profile of v4, /device:TPU:1, one launch (start us, length us, event | category | flops | bytes accessed | tf_op | source)
XLA Modules:
  0.0 70.3 jit_solution(5644978408726346887)
XLA Ops:
  0.0 69.1 %shard_map.28 = f32[1,512]{1,0:T(1,128)} custom-call(s32[1,512]{1,0:T(1,128)} %bitcast.3, bf16[512,768]{1,0:T(8,128)(2,1)} %embed_ref.1), custom_call_target="tpu_custom_call" | custom-call | tf_op jit(solution)/shard_map/pallas_call | solution.py:362
  69.1 1.3 %copy.4 = f32[512]{0:T(512)} copy(f32[512]{0:T(512)} %bitcast.2) | data formatting | bytes 4096

commit v5 on v4

--- a/solution.py
+++ b/solution.py
@@ -49,9 +49,9 @@
 def kernel(
     nz, side, cap,
     cluster_ref, embed_ref, out_ref,
-    cluster_rows, embed, unit, send, lined, ring, own, peer, best, reply, relay, home,
+    cluster_rows, embed, unit, send, lined, ring, own, peer, best, reply, home,
     fetch_sem, line_send, line_recv, ring_send, ring_recv, plane_send, plane_recv,
-    swap_send, swap_recv, reply_send, relay_recv, home_recv,
+    swap_send, swap_recv, reply_send, home_recv,
 ):
     rows, width = embed.shape
     far = nz // 2
@@ -88,7 +88,7 @@
     fetch_embed.start()
 
     barrier = pltpu.get_barrier_semaphore()
-    partners = [device(z_at[o], a, b) for o in range(1, nz)]
+    partners = [device(z_at[o], a, b) for o in (1, nz - 1)]
     partners += [device(z, a_at[oa], b_at[ob]) for oa, ob in others]
     partners += [peer_device]
     for partner in partners:
@@ -297,34 +297,26 @@
         result = jnp.maximum(result / width, -1.0)
         for piece in range(pieces):
             reply[:, piece] = result[:, :, piece * LANES:(piece + 1) * LANES]
-        slab = relay.at[:, lax.div(z, 2)]
-        for o in range(1, nz):
-            pltpu.make_async_remote_copy(
-                reply.at[z_at[o]], slab, reply_send, relay_recv,
-                device_id=device(z_at[o], a, b), device_id_type=MESH,
-            ).start()
-        pltpu.make_async_copy(reply.at[z], slab, relay_recv).start()
-
-    wait_for(relay, relay_recv)
-    for oa, ob in others:
-        target = b_at[ob] * side + a_at[oa]
-        pltpu.make_async_remote_copy(
-            relay.at[lax.div(target, group)], home.at[place], reply_send, home_recv,
-            device_id=device(z, a_at[oa], b_at[ob]), device_id_type=MESH,
-        ).start()
-    pltpu.make_async_copy(relay.at[lax.div(place, group)], home.at[place], home_recv).start()
-
-    entry = iota((owners, 1), 0)
-    from_place, level = lax.div(entry, far), lax.rem(entry, far)
-    from_b, from_a = lax.div(from_place, side), lax.rem(from_place, side)
-    from_z = 2 * level + lax.rem(from_a + from_b, 2)
-    held = (from_z * side + from_a) * per_line + lax.div(from_b, 2)
-    wanted = jnp.where(held == owner, 1.0, 0.0)
+        landing = home.at[(z * side + a) * per_line + lax.div(b, 2)]
+        for oz in sorted(range(nz), key=lambda o: -min(o, nz - o)):
+            for oa in range(side):
+                for ob in range(side):
+                    if (oz, oa, ob) == (0, 0, 0):
+                        continue
+                    target = b_at[ob] * side + a_at[oa]
+                    pltpu.make_async_remote_copy(
+                        reply.at[z_at[oz], lax.div(target, group)], landing,
+                        reply_send, home_recv,
+                        device_id=device(z_at[oz], a_at[oa], b_at[ob]), device_id_type=MESH,
+                    ).start()
+        pltpu.make_async_copy(reply.at[z, lax.div(place, group)], landing, home_recv).start()
+
     lane = lax.rem(place, group) * cap + rank
-    wait_for(home, home_recv)
-    answers = home[...].reshape(owners, LANES)
+    answered = home.at[pl.ds(0, owners)]
+    wait_for(answered, home_recv)
+    answers = answered[...].reshape(owners, LANES)
     picked = lax.dot_general(
-        answers, wanted, (((0,), (0,)), ((), ())),
+        answers, named, (((0,), (0,)), ((), ())),
         preferred_element_type=F32, precision=lax.Precision.HIGHEST,
     )
     out_ref[...] = jnp.sum(
@@ -336,15 +328,12 @@
     for direction in range(2):
         sent = ring.at[direction]
         wait_for(sent, ring_send)
-    replied = home.at[pl.ds(0, places - 1)]
-    wait_for(replied, reply_send)
 
     @pl.when(is_owner)
     def _():
         passed = 2 * (side * per_line - 1) + (nz - 2) * side * (per_line - 1)
         wait_for(own.at[pl.ds(0, passed)], plane_send)
-        told = reply.at[pl.ds(0, nz - 1)]
-        wait_for(told, reply_send)
+        wait_for(home.at[pl.ds(0, nz * places - 1)], reply_send)
         for zs in range(nz):
             wait_for(plane(own, zs), swap_send.at[zs])
 
@@ -375,8 +364,7 @@
             pltpu.VMEM((nz * places, cap, width), BF16),
             pltpu.VMEM((nz, 8, places * cap), F32),
             pltpu.VMEM((nz, pieces, 1, LANES), F32),
-            pltpu.VMEM((pieces, nz // 2, 1, LANES), F32),
-            pltpu.VMEM((places, nz // 2, 1, LANES), F32),
+            pltpu.VMEM((nz * places, 1, LANES), F32),
             pltpu.SemaphoreType.DMA((2,)),
             pltpu.SemaphoreType.DMA,
             pltpu.SemaphoreType.DMA((nz,)),
@@ -388,12 +376,14 @@
             pltpu.SemaphoreType.DMA((nz,)),
             pltpu.SemaphoreType.DMA,
             pltpu.SemaphoreType.DMA,
-            pltpu.SemaphoreType.DMA,
         ],
         compiler_params=pltpu.CompilerParams(
-            collective_id=0, has_side_effects=True, vmem_limit_bytes=(64 * 1024 - 512) * 1024
+            collective_id=0, has_side_effects=True, vmem_limit_bytes=40 * 1024 * 1024
         ),
-    )(cluster.reshape(1, rows), embed)
+    )(
+        pltpu.with_memory_space_constraint(cluster.reshape(1, rows), pltpu.HBM),
+        pltpu.with_memory_space_constraint(embed, pltpu.HBM),
+    )
     return out.reshape(rows)
 
 

time: 70.4 us -> 65.7 us (0.933)
  Pallas kernels: 69.1 us -> 65 us
    pallas_call x1, Pallas kernels: 69.1 us -> 65 us  [on_device(): pl.pallas_call(functools.partial(kernel, nz, side, cap), out_shape=jax.Sh...]
where the time goes in v5:
time: 65.7 us; the launch traced here: 65.6 us
  Pallas kernels  65 us (99%)
    pallas_call x1, Pallas kernels, on_device(): pl.pallas_call(functools.partial(kernel, nz, side, cap), out_shape=jax.Sh...  65 us

profile of v5, /device:TPU:1, one launch (start us, length us, event | category | flops | bytes accessed | tf_op | source)
XLA Modules:
  0.0 65.6 jit_solution(3014930884642932275)
XLA Ops:
  0.0 65.0 %shard_map.28 = f32[1,512]{1,0:T(1,128)S(1)} custom-call(s32[1,512]{1,0:T(1,128)} %bitcast.3, bf16[512,768]{1,0:T(8,128)(2,1)} %embed_ref.1), custom_call_target="tpu_custom_call" | custom-call | tf_op jit(solution)/shard_map/pallas_call | solution.py:351
  65.0 0.6 copy.4

commit v6 on v5

--- a/solution.py
+++ b/solution.py
@@ -27,21 +27,26 @@
 
 
 RING_ORDER = {
-    2: ((2, 1, None), (1, 1, 0), (2, 2, None), (1, 1, 1)),
+    2: ((2, 1, 0, 1), (1, 1, 0, 1), (2, 2, 0, 1), (1, 1, 1, 1)),
     4: (
-        (1, 1, 0), (1, 1, 1), (2, 1, 0), (2, 1, 1), (2, 2, 0), (3, 1, 0), (2, 2, 1), (3, 2, 0),
-        (4, 1, None), (3, 1, 1), (4, 2, None), (3, 3, 0), (3, 2, 1), (4, 3, None), (3, 3, 1),
-        (4, 4, None),
+        (1, 1, 0, 2), (1, 1, 2, 2), (2, 1, 0, 2), (2, 1, 2, 2), (3, 1, 0, 2), (2, 2, 0, 2),
+        (2, 2, 2, 2), (3, 1, 2, 2), (3, 2, 0, 2), (4, 1, 0, 1), (4, 1, 1, 1), (3, 2, 2, 2),
+        (3, 3, 0, 2), (4, 2, 0, 1), (4, 2, 1, 1), (3, 3, 2, 1), (4, 3, 0, 1), (4, 3, 1, 1),
+        (3, 3, 3, 1), (4, 4, 0, 1), (4, 4, 1, 1),
     ),
 }
 AHEAD = 4
 SPREAD_HERE = 5
 OWNER_WORK = {
-    2: ((4, "meet", 0, 2), (4, "own", 0, 2), (4, "peer", 0, 2)),
+    2: (
+        (4, "meet", 0, 2), (4, "own", 0, 2), (4, "peer", 0, 2),
+        (4, "meet", 3, 3), (4, "own", 3, 3), (4, "peer", 3, 3),
+    ),
     4: (
         (8, "meet", 0, 2), (9, "own", 0, 2), (10, "peer", 0, 2),
-        (11, "meet", 3, 4), (12, "own", 3, 4), (14, "peer", 3, 4),
-        (16, "meet", 5, 6), (16, "own", 5, 6),
+        (12, "meet", 3, 4), (13, "own", 3, 4), (15, "peer", 3, 4),
+        (21, "meet", 5, 6), (21, "own", 5, 6), (21, "peer", 5, 5), (21, "meet", 7, 7),
+        (21, "peer", 6, 6), (21, "own", 7, 7), (21, "peer", 7, 7),
     ),
 }
 
@@ -120,7 +125,6 @@
         send[pl.ds(zo * side, side)] = packed.reshape(side, per_line, cap, width)
 
     def line_up(zo):
-        pack(zo)
         for o in range(1, side):
             pltpu.make_async_remote_copy(
                 send.at[zo * side + a_at[o]], lined.at[zo, a], line_send, line_recv.at[zo],
@@ -130,19 +134,33 @@
             send.at[zo * side + a], lined.at[zo, a], line_recv.at[zo]
         ).start()
 
+    def first_of(direction, message):
+        return message[2] + (direction * per_line if message[0] == far else 0)
+
+    def held_by(direction, index):
+        return ring.at[direction, index, pl.ds(0, order[index][3])]
+
+    def before(index):
+        d, h, first, count = order[index]
+        for i, (e, hop, start, held) in enumerate(order):
+            if (e, hop) == (d, h - 1) and start <= first and first + count <= start + held:
+                return i, first - start
+        return -1, 0
+
     def pass_on(direction, index):
-        d, h, u = order[index]
-        if h == 1:
+        d, h, _, count = order[index]
+        if h > 1:
+            source, start = before(index)
+            source = ring.at[direction, source, pl.ds(start, count)]
+        else:
             zo = z_at[d if direction == 0 else nz - d]
-            first = per_line * (direction if u is None else u)
+            first = first_of(direction, order[index])
             if d == 1:
-                source = send.at[pl.ds(zo * side + first, per_line)]
+                source = send.at[pl.ds(zo * side + first, count)]
             else:
-                source = lined.at[zo, pl.ds(first, per_line)]
-        else:
-            source = ring.at[direction, order.index((d, h - 1, u))]
+                source = lined.at[zo, pl.ds(first, count)]
         pltpu.make_async_remote_copy(
-            source, ring.at[direction, index], ring_send, ring_recv.at[direction, index],
+            source, held_by(direction, index), ring_send, ring_recv.at[direction, index],
             device_id=device(z_at[1 if direction == 0 else nz - 1], a, b), device_id_type=MESH,
         ).start()
 
@@ -239,58 +257,52 @@
                     wait_for(plane(peer, zs), swap_recv.at[zs])
                 against(peer, 1 - core, first, last)
 
-    ready = [0 if h == 1 else order.index((d, h - 1, u)) + 1 for d, h, u in order]
+    ready = [before(i)[0] + 1 if h > 1 else min(1, d // 3) for i, (d, h, _, _) in enumerate(order)]
     begins = [max(0, i + 1 - AHEAD, r) for i, r in enumerate(ready)]
     for i in range(1, len(begins)):
         begins[i] = max(begins[i], begins[i - 1])
     waited = set()
-    sent_first = [order.index((1, 1, u)) for u in range(2 if far > 2 else 1)]
+    sent_first = [i for i in range(2) if order[i][0] == 1]
 
     def line_ready(offset):
         if offset not in waited:
             waited.add(offset)
             wait_for(lined.at[z_at[offset]], line_recv.at[z_at[offset]])
 
-    def send_after(count):
-        for index, (d, h, _) in enumerate(order):
+    def send_after(count, direction):
+        for index, (d, h, _, _) in enumerate(order):
             if begins[index] == count and index not in sent_first:
-                for direction in range(2):
-                    if h == 1 and d > 1:
-                        line_ready(d if direction == 0 else nz - d)
-                    pass_on(direction, index)
+                if h == 1 and d > 1:
+                    line_ready(d if direction == 0 else nz - d)
+                pass_on(direction, index)
 
     pl.semaphore_wait(barrier, len(partners))
     for offset in (1, nz - 1):
         pack(z_at[offset])
-        for index in range(2 if far > 2 else 1):
-            pass_on(0 if offset == 1 else 1, order.index((1, 1, index)))
+        for index in sent_first:
+            pass_on(0 if offset == 1 else 1, index)
     for offset in [sign * d % nz for d in range(2, far) for sign in (1, -1)] + [far, 0]:
+        pack(z_at[offset])
         line_up(z_at[offset])
-    send_after(0)
+    for direction in range(2):
+        send_after(0, direction)
     best[...] = jnp.full(best.shape, -float(width), F32)
     for count, message in enumerate(order, 1):
-        d, h, u = message
+        d, h, _, _ = message
         for direction in range(2):
-            buffer = ring.at[direction, count - 1]
+            buffer = held_by(direction, count - 1)
             wait_for(buffer, ring_recv.at[direction, count - 1])
+            send_after(count, direction)
             if h == d:
                 zs = z_at[nz - d if direction == 0 else d]
-                first = per_line * (direction if u is None else u)
+                first = first_of(direction, message)
                 (spread_near if d == 1 else spread)(buffer, first, zs)
-        send_after(count)
         if count == min(SPREAD_HERE, len(order)):
             line_ready(0)
             spread(lined.at[z], 0, z)
         for after, what, first, last in OWNER_WORK[far]:
             if after == count:
                 work(what, first, last)
-    last = nz - 1
-    work("meet", last, last)
-    if far > 2:
-        work("peer", last - 2, last - 1)
-    work("own", last, last)
-    work("peer", last, last)
-
     @pl.when(is_owner)
     def _():
         result = jnp.max(best[...], axis=1, keepdims=True)
@@ -312,12 +324,17 @@
         pltpu.make_async_copy(reply.at[z, lax.div(place, group)], landing, home_recv).start()
 
     lane = lax.rem(place, group) * cap + rank
+    wanted = jnp.concatenate([named.astype(BF16)] * 3, axis=0)
     answered = home.at[pl.ds(0, owners)]
     wait_for(answered, home_recv)
-    answers = answered[...].reshape(owners, LANES)
+    left = answered[...].reshape(owners, LANES)
+    split = []
+    for _ in range(3):
+        split.append(left.astype(BF16))
+        left = left - split[-1].astype(F32)
     picked = lax.dot_general(
-        answers, named, (((0,), (0,)), ((), ())),
-        preferred_element_type=F32, precision=lax.Precision.HIGHEST,
+        jnp.concatenate(split, axis=0), wanted, (((0,), (0,)), ((), ())),
+        preferred_element_type=F32,
     )
     out_ref[...] = jnp.sum(
         jnp.where(iota((LANES, rows), 0) == lane, picked, 0.0), axis=0, keepdims=True
@@ -326,8 +343,8 @@
     lines = send.at[pl.ds(0, (nz - 2) * (side - 1))]
     wait_for(lines, line_send)
     for direction in range(2):
-        sent = ring.at[direction]
-        wait_for(sent, ring_send)
+        parts = sum(message[3] for message in order) // per_line
+        wait_for(ring.at[direction, pl.ds(0, parts)], ring_send)
 
     @pl.when(is_owner)
     def _():

time: 65.7 us -> 64.6 us (0.983)
  Pallas kernels: 65 us -> 64 us
    pallas_call x1, Pallas kernels: 65 us -> 64 us  [on_device(): pl.pallas_call(functools.partial(kernel, nz, side, cap), out_shape=jax.Sh...]
where the time goes in v6:
time: 64.6 us
  Pallas kernels  64 us (99%)
    pallas_call x1, Pallas kernels, on_device(): pl.pallas_call(functools.partial(kernel, nz, side, cap), out_shape=jax.Sh...  64 us

profile of v6, /device:TPU:1, one launch (start us, length us, event | category | flops | bytes accessed | tf_op | source)
XLA Modules:
  0.0 64.6 jit_solution(7383997476064953059)
XLA Ops:
  0.0 64.0 %shard_map.28 = f32[1,512]{1,0:T(1,128)S(1)} custom-call(s32[1,512]{1,0:T(1,128)} %bitcast.3, bf16[512,768]{1,0:T(8,128)(2,1)} %embed_ref.1), custom_call_target="tpu_custom_call" | custom-call | tf_op jit(solution)/shard_map/pallas_call | solution.py:368
  64.0 0.6 copy.4

commit v7 on v6

--- a/solution.py
+++ b/solution.py
@@ -43,8 +43,8 @@
         (4, "meet", 3, 3), (4, "own", 3, 3), (4, "peer", 3, 3),
     ),
     4: (
-        (8, "meet", 0, 2), (9, "own", 0, 2), (10, "peer", 0, 2),
-        (12, "meet", 3, 4), (13, "own", 3, 4), (15, "peer", 3, 4),
+        (6, "meet", 0, 2), (7, "own", 0, 2), (8, "peer", 0, 2),
+        (9, "meet", 3, 4), (10, "own", 3, 4), (12, "peer", 3, 4),
         (21, "meet", 5, 6), (21, "own", 5, 6), (21, "peer", 5, 5), (21, "meet", 7, 7),
         (21, "peer", 6, 6), (21, "own", 7, 7), (21, "peer", 7, 7),
     ),

time: 64.6 us -> 63.8 us (0.988)
  Pallas kernels: 64 us -> 63.1 us
    pallas_call x1, Pallas kernels: 64 us -> 63.1 us  [on_device(): pl.pallas_call(functools.partial(kernel, nz, side, cap), out_shape=jax.Sh...]
where the time goes in v7:
time: 63.8 us; the launch traced here: 63.7 us
  Pallas kernels  63.1 us (99%)
    pallas_call x1, Pallas kernels, on_device(): pl.pallas_call(functools.partial(kernel, nz, side, cap), out_shape=jax.Sh...  63.1 us

profile of v7, /device:TPU:1, one launch (start us, length us, event | category | flops | bytes accessed | tf_op | source)
XLA Modules:
  0.0 63.7 jit_solution(11429394224987953775)
XLA Ops:
  0.0 63.1 %shard_map.28 = f32[1,512]{1,0:T(1,128)S(1)} custom-call(s32[1,512]{1,0:T(1,128)} %bitcast.3, bf16[512,768]{1,0:T(8,128)(2,1)} %embed_ref.1), custom_call_target="tpu_custom_call" | custom-call | tf_op jit(solution)/shard_map/pallas_call | solution.py:368
  63.1 0.6 copy.4

commit v8 on v7

--- a/solution.py
+++ b/solution.py
@@ -44,7 +44,7 @@
     ),
     4: (
         (6, "meet", 0, 2), (7, "own", 0, 2), (8, "peer", 0, 2),
-        (9, "meet", 3, 4), (10, "own", 3, 4), (12, "peer", 3, 4),
+        (9, "meet", 3, 4), (9, "own", 3, 4), (11, "peer", 3, 4),
         (21, "meet", 5, 6), (21, "own", 5, 6), (21, "peer", 5, 5), (21, "meet", 7, 7),
         (21, "peer", 6, 6), (21, "own", 7, 7), (21, "peer", 7, 7),
     ),
@@ -259,6 +259,8 @@
 
     ready = [before(i)[0] + 1 if h > 1 else min(1, d // 3) for i, (d, h, _, _) in enumerate(order)]
     begins = [max(0, i + 1 - AHEAD, r) for i, r in enumerate(ready)]
+    if far > 2:
+        begins[3] = 1
     for i in range(1, len(begins)):
         begins[i] = max(begins[i], begins[i - 1])
     waited = set()

time: 63.8 us -> 64 us (level)
  no operation moved by 1% of the time
where the time goes in v8:
time: 64 us; the launch traced here: 63.9 us
  Pallas kernels  63.3 us (99%)
    pallas_call x1, Pallas kernels, on_device(): pl.pallas_call(functools.partial(kernel, nz, side, cap), out_shape=jax.Sh...  63.3 us

profile of v8, /device:TPU:1, one launch (start us, length us, event | category | flops | bytes accessed | tf_op | source)
XLA Modules:
  0.0 63.9 jit_solution(15011101643565190649)
XLA Ops:
  0.0 63.3 %shard_map.28 = f32[1,512]{1,0:T(1,128)S(1)} custom-call(s32[1,512]{1,0:T(1,128)} %bitcast.3, bf16[512,768]{1,0:T(8,128)(2,1)} %embed_ref.1), custom_call_target="tpu_custom_call" | custom-call | tf_op jit(solution)/shard_map/pallas_call | solution.py:370
  63.3 0.6 copy.4

commit v9 on v8

--- a/solution.py
+++ b/solution.py
@@ -45,8 +45,8 @@
     4: (
         (6, "meet", 0, 2), (7, "own", 0, 2), (8, "peer", 0, 2),
         (9, "meet", 3, 4), (9, "own", 3, 4), (11, "peer", 3, 4),
-        (21, "meet", 5, 6), (21, "own", 5, 6), (21, "peer", 5, 5), (21, "meet", 7, 7),
-        (21, "peer", 6, 6), (21, "own", 7, 7), (21, "peer", 7, 7),
+        (21, "meet", 5, 6), (21, "own", 5, 6), (21, "meet", 7, 7), (21, "own", 7, 7),
+        (21, "peer", 5, 6), (21, "peer", 7, 7),
     ),
 }
 

time: 64 us -> 63.7 us (level)
  no operation moved by 1% of the time
where the time goes in v9:
time: 63.7 us; the launch traced here: 63.4 us
  Pallas kernels  62.8 us (99%)
    pallas_call x1, Pallas kernels, on_device(): pl.pallas_call(functools.partial(kernel, nz, side, cap), out_shape=jax.Sh...  62.8 us

profile of v9, /device:TPU:1, one launch (start us, length us, event | category | flops | bytes accessed | tf_op | source)
XLA Modules:
  0.0 63.4 jit_solution(10428522226318749444)
XLA Ops:
  0.0 62.8 %shard_map.28 = f32[1,512]{1,0:T(1,128)S(1)} custom-call(s32[1,512]{1,0:T(1,128)} %bitcast.3, bf16[512,768]{1,0:T(8,128)(2,1)} %embed_ref.1), custom_call_target="tpu_custom_call" | custom-call | tf_op jit(solution)/shard_map/pallas_call | solution.py:370
  62.8 0.6 copy.4
